TPU v7x, 32 devices: a whole 2x2x4 slice. The times are simulated.
32 devices in a mesh: frame: 2 (over x), rows: 16 (over z, y, core).
Axes of the slice: x: 2, y: 2, z: 4, core: 2. Of those that a mesh axis runs over, the one named last changes fastest.
Arguments:
- interferograms: bfloat16 [600, 256, 256], P(None, ('frame', 'rows')), parts along dimension 1, may hold values from -6 to 6
- pseudo_inverse: bfloat16 [200, 600], replicated, may hold values from -0.25 to 0.25
- date_pairs: int32 [2, 600], replicated, may hold values from 0 to 199, as said below
- ref_pixel: int32 [2], P('frame'), parts along dimension 0, may hold values from 0 to 32767
- band_width: int32 [1], replicated, may hold values from 5 to 60
- prior_mean: float32 [32, 4, 2048], P(('frame', 'rows')), parts along dimension 0, may hold values from -6 to 6
- prior_precision: float32 [32, 4, 2048], P(('frame', 'rows')), parts along dimension 0, may hold values from 20 to 200
Outputs:
- series: bfloat16 [32, 200, 2048], P(('frame', 'rows')), parts along dimension 0
- kalman_state: float32 [32, 4, 2048], P(('frame', 'rows')), parts along dimension 0
- misfit: bfloat16 [32, 2048], P(('frame', 'rows')), parts along dimension 0
There are 2 independent parts, one for each index of `frame`. A program takes and returns all parts, laid end to end along the dimension named above; an argument that names none is the same for every part. Nothing has to cross between parts.
Inputs may be any that keep to these rules, and one draw needn't show every extreme that they name: `date_pairs`: row 0 holds each interferogram's earlier date, row 1 its later date, 1 to 6 dates after the earlier one; some interferogram starts on the first date and some ends on the last.
All inputs are finite; a program needn't handle non-finite values.
Results may differ from a plain program's by a relative error of at most 0.0017.
The roundings to bfloat16 on the way count: a program that leaves them out, or rounds other values in their place, can miss the bound.
Values may be sent and summed in bfloat16 or wider, within the bound.
A program may use at most 64 MiB of HBM per device.

v0:
```python
import math

import jax
import jax.numpy as jnp
from jax import lax
from jax.sharding import PartitionSpec as P

DATES = 200
RADIUS = 4


def padded_2(cells, sides, width):
    for axis, dim in sides:
        count = lax.axis_size(axis)
        ends = count - 1
        head = lax.slice_in_dim(cells, 0, width, axis=dim)
        tail = lax.slice_in_dim(cells, cells.shape[dim] - width, cells.shape[dim], axis=dim)
        cells = jnp.concatenate(
            [
                lax.ppermute(tail, axis, [(i, (i + 1) % count) for i in range(ends)]),
                cells,
                lax.ppermute(head, axis, [((i + 1) % count, i) for i in range(ends)]),
            ],
            axis=dim,
        )
    return cells


def filter_taps(band_width):
    spread = band_width[0].astype(jnp.float32) / 10.0
    offsets = jnp.arange(-RADIUS, RADIUS + 1).astype(jnp.float32)
    raw_taps = jnp.exp(-offsets * offsets / (2.0 * spread * spread))
    return raw_taps / jnp.sum(raw_taps)


def column_pass(images, kernel_taps):
    values = images.astype(jnp.float32)
    columns = values.shape[2]
    padded = jnp.pad(values, ((0, 0), (0, 0), (RADIUS, RADIUS)))
    summed = kernel_taps[0] * padded[:, :, 0:columns]
    for offset in range(1, 2 * RADIUS + 1):
        summed = summed + kernel_taps[offset] * padded[:, :, offset : offset + columns]
    return summed.astype(jnp.bfloat16)


def row_pass(extended, kernel_taps, height):
    summed = kernel_taps[0] * extended[:, 0:height]
    for offset in range(1, 2 * RADIUS + 1):
        summed = summed + kernel_taps[offset] * extended[:, offset : offset + height]
    return summed


def design_of(date_pairs):
    date_index = jnp.arange(DATES, dtype=jnp.int32)
    later_date = (date_index[None, :] == date_pairs[1][:, None]).astype(jnp.float32)
    earlier = (date_index[None, :] == date_pairs[0][:, None]).astype(jnp.float32)
    return (later_date - earlier).astype(jnp.bfloat16)


def trend_basis():
    epochs = jnp.arange(DATES).astype(jnp.float32)
    centred = (epochs - (DATES - 1) / 2.0) / DATES
    annual_phase = 2.0 * math.pi * 12.0 / 365.25 * epochs
    constant = jnp.ones_like(epochs)
    return jnp.stack([constant, centred, jnp.cos(annual_phase), jnp.sin(annual_phase)], axis=1)


def misfit_of(slab_values, displacement, design):
    modelled = jnp.dot(design, displacement, preferred_element_type=jnp.float32)
    residual = slab_values.astype(jnp.float32) - modelled
    return jnp.mean(residual * residual, axis=0).astype(jnp.bfloat16)


def slab_major(values, slab_count, slab_cols):
    leading, local_rows, columns = values.shape
    split_up = values.reshape(leading, local_rows, slab_count, slab_cols).transpose(2, 0, 1, 3)
    return split_up.reshape(slab_count, leading, local_rows * slab_cols)


def from_sources(arrived):
    sources, leading, piece_len = arrived.shape
    return arrived.transpose(1, 0, 2).reshape(leading, sources * piece_len)


def solve_small(matrix, right_side):
    dimension = len(right_side)
    factor = [[None] * dimension for row_at in range(dimension)]
    for column_at in range(dimension):
        pivot_sq = matrix[column_at][column_at]
        for term_at in range(column_at):
            pivot_sq = pivot_sq - factor[column_at][term_at] * factor[column_at][term_at]
        factor[column_at][column_at] = jnp.sqrt(pivot_sq)
        for row_at in range(column_at + 1, dimension):
            element = matrix[row_at][column_at]
            for term_at in range(column_at):
                element = element - factor[row_at][term_at] * factor[column_at][term_at]
            factor[row_at][column_at] = element / factor[column_at][column_at]
    forward = []
    for row_at in range(dimension):
        element = right_side[row_at]
        for term_at in range(row_at):
            element = element - factor[row_at][term_at] * forward[term_at]
        forward.append(element / factor[row_at][row_at])
    solution = [None] * dimension
    for row_at in reversed(range(dimension)):
        element = forward[row_at]
        for term_at in range(row_at + 1, dimension):
            element = element - factor[term_at][row_at] * solution[term_at]
        solution[row_at] = element / factor[row_at][row_at]
    return solution


def kalman_update(series, misfit, prior_mean, prior_precision):
    trend_rows = trend_basis()
    trend_gram = jnp.dot(trend_rows.T, trend_rows, precision=lax.Precision.HIGHEST)
    projected = jnp.dot(trend_rows.T, series.astype(jnp.float32), precision=lax.Precision.HIGHEST)
    inverse_noise = 1.0 / (0.1 + misfit.astype(jnp.float32))
    matrix = [
        [
            trend_gram[row_at, column_at] * inverse_noise
            + (prior_precision[row_at] if row_at == column_at else 0.0)
            for column_at in range(4)
        ]
        for row_at in range(4)
    ]
    right_side = [
        prior_precision[row_at] * prior_mean[row_at] + projected[row_at] * inverse_noise
        for row_at in range(4)
    ]
    return jnp.stack(solve_small(matrix, right_side), axis=0)


def on_device(
    interferograms, pseudo_inverse, date_pairs, ref_pixel, band_width, prior_mean, prior_precision
):
    kernel_taps = filter_taps(band_width)
    slab_count = lax.axis_size("rows")
    image_count, local_rows, columns = interferograms.shape
    slab_cols = columns // slab_count
    extended = padded_2(interferograms, (("rows", 1),), RADIUS)
    smoothed = column_pass(extended, kernel_taps)
    smoothed = lax.optimization_barrier(smoothed)
    lowpass = row_pass(smoothed.astype(jnp.float32), kernel_taps, local_rows)
    filtered = (interferograms.astype(jnp.float32) - lowpass).astype(jnp.bfloat16)
    design = design_of(date_pairs)
    arrived = lax.all_to_all(
        slab_major(filtered, slab_count, slab_cols), "rows", split_axis=0, concat_axis=0, tiled=True
    )
    slab_values = from_sources(arrived)
    displacement = jnp.dot(pseudo_inverse, slab_values, preferred_element_type=jnp.float32).astype(
        jnp.bfloat16
    )
    misfit = misfit_of(slab_values, displacement, design)
    ref_index = ref_pixel[0]
    ref_row = ref_index // columns
    ref_col = ref_index % columns
    owner_slab = ref_col // slab_cols
    local_pixel = ref_row * slab_cols + ref_col - owner_slab * slab_cols
    own_series = lax.dynamic_slice_in_dim(displacement, local_pixel, 1, 1)[:, 0]
    own_term = jnp.where(lax.axis_index("rows") == owner_slab, own_series.astype(jnp.float32), 0.0)
    ref_series = lax.psum(own_term, "rows")
    series = (displacement.astype(jnp.float32) - ref_series[:, None]).astype(jnp.bfloat16)
    kalman_state = kalman_update(series, misfit, prior_mean[0], prior_precision[0])
    return (series[None], kalman_state[None], misfit[None])


def solution(mesh):
    placed = (
        P(None, ("frame", "rows"), None),
        P(),
        P(),
        P("frame"),
        P(),
        P(("frame", "rows"), None, None),
        P(("frame", "rows"), None, None),
    )
    return jax.shard_map(
        on_device,
        mesh=mesh,
        in_specs=placed,
        out_specs=(
            P(("frame", "rows"), None, None),
            P(("frame", "rows"), None, None),
            P(("frame", "rows"), None),
        ),
        check_vma=False,
    )
```

profile of v0, /device:TPU:0, one launch (start us, length us, event | category | flops | bytes accessed | tf_op | source)
XLA Modules:
  0.0 244.6 jit_solution(715240647253076947)
XLA Ops:
  0.6 0.0 copy-start
  0.6 3.5 %fusion.42 = (bf16[600,4,256]{2,1,0:T(4,128)(2,1)S(1)}, bf16[600,4,256]{2,1,0:T(4,128)(2,1)S(1)}) fusion(bf16[600,8,256]{2,1,0:T(8,128)(2,1)} %param.7), kind=kLoop, calls=%fused_computation.103 | loop fusion | bytes 4915200 | tf_op jit(solution)/shard_map/slice | solution.py:17
  4.1 1.2 copy.26
  5.3 3.4 %collective-permute-start = (bf16[600,4,256]{2,0,1:T(8,128)(2,1)}, bf16[600,4,256]{2,0,1:T(8,128)(2,1)}, u32[]{:S(2)}, u32[]{:S(2)}) collective-permute-start(bf16[600,4,256]{2,0,1:T(8,128)(2,1)} %copy.26), channel_id=1, source_target_pairs={{0,1},{1,2},{2,3},{3,4},{4,5},{5,6},{6,7},{7,8},{8,9},{9,10},{10,1... | collective-permute-start | bytes 3686408 | tf_op jit(solution)/shard_map/ppermute | solution.py:20
  8.7 1.2 copy.27
  9.9 1.3 collective-permute-start.1
  11.2 3.8 %copy.17 = bf16[600,8,256]{0,2,1:T(8,128)(2,1)S(1)} copy(bf16[600,8,256]{2,1,0:T(8,128)(2,1)} %param.7) | data formatting | bytes 4915200 | tf_op args[0]
  15.7 0.6 fusion.38
  16.3 0.7 broadcast_divide_fusion
  17.0 0.7 fusion.44
  17.7 0.0 collective-permute-done
  17.7 2.4 copy.20
  20.1 0.0 collective-permute-done.1
  20.1 2.4 %copy.22 = bf16[600,4,256]{0,2,1:T(8,128)(2,1)} copy(bf16[600,4,256]{2,0,1:T(8,128)(2,1)} %collective-permute-done.1) | data formatting | bytes 2457600 | tf_op jit(solution)/shard_map/ppermute | solution.py:22
  22.5 6.6 %maximum_convert_fusion = f32[600,16,256]{0,2,1:T(8,128)} fusion(bf16[600,4,256]{0,2,1:T(8,128)(2,1)} %copy.22, bf16[600,8,256]{0,2,1:T(8,128)(2,1)S(1)} %copy.17, bf16[600,4,256]{0,2,1:T(8,128)(2,1)} %copy.20), kind=kLoop, calls=%fused_computation.28 | loop fusion | flops 7372800 | bytes 14745600 | tf_op jit(solution)/shard_map/convert_element_type | solution.py:37
  29.1 46.9 %add_convert_fusion = bf16[600,16,256]{0,2,1:T(8,128)(2,1)} fusion(f32[600,16,256]{0,2,1:T(8,128)} %maximum_convert_fusion, f32[]{:T(128)} %bitcast.9, f32[]{:T(128)} %bitcast.8, f32[]{:T(128)} %bitcast.7, f32[]{:T(128)} %bitcast.6, f32[]{:T(128)} %bitcast.5, f32[]{:T(128)} %bitcast.4, f32[]{:T(128)} %bitcast.3, f32[]{:T(128)} %bitcast.2, f32[]{:T(128)} %bitcast.1), kind=kLoop, calls=%fused_computation | loop fusion | flops 44236800 | bytes 14745636 | tf_op jit(solution)/shard_map/convert_element_type | solution.py:43
  76.0 7.6 %convert_element_type.176 = f32[600,16,256]{0,2,1:T(8,128)} convert(bf16[600,16,256]{0,2,1:T(8,128)(2,1)} %add_convert_fusion) | non-fusion elementwise | flops 2457600 | bytes 14745600 | tf_op jit(solution)/shard_map/convert_element_type | solution.py:143
  83.6 25.9 %fusion.7 = bf16[600,8,256]{0,2,1:T(8,128)(2,1)} fusion(f32[600,16,256]{0,2,1:T(8,128)} %convert_element_type.176, bf16[600,8,256]{0,2,1:T(8,128)(2,1)S(1)} %copy.17, f32[]{:T(128)} %bitcast.9, f32[]{:T(128)} %bitcast.8, f32[]{:T(128)} %bitcast.7, f32[]{:T(128)} %bitcast.6, f32[]{:T(128)} %bitcast.5, f32[]{:T(128)} %bitcast.4, f32[]{:T(128)} %bitcast.3, ...), kind=kLoop, calls=%fused_computation.12 | loop fusion | flops 24576000 | bytes 49152036 | tf_op jit(solution)/shard_map/convert_element_type | solution.py:144
  109.5 2.1 copy.23
  111.6 0.0 copy-start.3
  111.6 2.6 %copy.24 = bf16[16,600,128]{2,1,0:T(8,128)(2,1)} copy(bf16[16,600,128]{1,2,0:T(8,128)(2,1)S(1)} %bitcast.159) | data formatting | bytes 4915200 | tf_op jit(solution)/shard_map/reshape | solution.py:77
  114.2 25.6 %all-to-all-start = ((bf16[16,600,128]{2,1,0:T(8,128)(2,1)}), bf16[16,600,128]{2,1,0:T(8,128)(2,1)S(1)}, u32[]{:S(2)}, u32[]{:S(2)}) async-start(bf16[16,600,128]{2,1,0:T(8,128)(2,1)} %copy.24), calls=%async_computation | async-start | bytes 4915200 | tf_op jit(solution)/shard_map/all_to_all | solution.py:146
  140.5 0.0 copy-start.6
  140.5 0.1 fusion.35
  140.5 0.0 copy-start.5
  140.5 0.1 add_multiply_fusion
  140.6 0.2 fusion.39
  140.8 0.7 fusion.43
  141.5 0.0 copy-done.6
  141.5 0.0 copy-done.5
  141.5 0.0 copy-done.3
  141.5 0.6 slice_reduce_fusion.1
  142.1 0.0 copy-start.4
  142.1 45.0 %all-to-all-done = bf16[16,600,128]{2,1,0:T(8,128)(2,1)S(1)} async-done(((bf16[16,600,128]{2,1,0:T(8,128)(2,1)}), bf16[16,600,128]{2,1,0:T(8,128)(2,1)S(1)}, u32[]{:S(2)}, u32[]{:S(2)}) %all-to-all-start) | async-done | bytes 2457632 | tf_op jit(solution)/shard_map/all_to_all | solution.py:146
  187.1 0.0 copy-done
  187.1 0.8 convolution_convert_fusion
  187.9 0.8 select_reduce_fusion
  188.7 40.8 %psum.7 = f32[200]{0:T(256)S(1)} all-reduce(f32[200]{0:T(256)} %select_reduce_fusion), channel_id=1, replica_groups=mesh['frame'=2,'rows'=16] {'rows'}, use_global_device_ids=true, to_apply=%region_1.2 | all-reduce | flops 200 | bytes 1600 | tf_op jit(solution)/shard_map/psum | solution.py:161
  229.5 1.2 fusion.17
  230.7 1.1 fusion.18
  231.8 0.0 copy-done.4
  231.8 0.0 copy-start.1
  231.8 0.0 copy-start.2
  231.8 1.0 multiply_reduce_fusion
  232.8 0.6 convert_element_type.189
  233.4 0.0 copy-done.1
  233.4 0.0 copy-done.2
  233.4 3.9 %subtract_divide_fusion.3 = (f32[1,2048]{1,0:T(1,128)S(1)}, f32[1,2048]{1,0:T(1,128)S(1)}, f32[1,2048]{1,0:T(1,128)S(1)}, f32[1,2048]{1,0:T(1,128)S(1)}, f32[1,2048]{1,0:T(1,128)S(1)}, /*index=5*/f32[1,2048]{1,0:T(1,128)S(1)}) fusion(f32[4,2048]{1,0:T(4,128)S(1)} %fusion.17, f32[1,4,2048]{2,1,0:T(4,128)S(1)} %copy-done.2, f32[1,4,2048]{2,1,0:T(4,128)S(1)} %copy-done.1, ...), kind=kLoop, calls=%fused_computation.74 | loop fusion | flops 92160 | bytes 127000 | tf_op jit(solution)/shard_map/div | solution.py:103
  237.3 6.6 %subtract_divide_fusion = (f32[1,2048]{1,0:T(1,128)S(1)}, f32[1,2048]{1,0:T(1,128)S(1)}, f32[1,2048]{1,0:T(1,128)S(1)}, f32[1,2048]{1,0:T(1,128)S(1)}) fusion(f32[1,2048]{1,0:T(1,128)S(1)} %get-tuple-element.11, f32[1,2048]{1,0:T(1,128)S(1)} %get-tuple-element.14, f32[]{:T(128)} %bitcast.25, f32[]{:T(128)} %bitcast.30, f32[]{:T(128)} %bitcast.20, ...), kind=kLoop, calls=%fused_computation.67 | loop fusion | flops 149504 | bytes 131112 | tf_op jit(solution)/shard_map/div | solution.py:109
  244.0 0.7 maximum_bitcast_fusion
  (2 shorter events, 0.0 us)
Async XLA Ops:
  0.6 186.5 %copy-start = (bf16[200,600]{1,0:T(8,128)(2,1)S(1)}, bf16[200,600]{1,0:T(8,128)(2,1)}, u32[]{:S(2)}) copy-start(bf16[200,600]{1,0:T(8,128)(2,1)} %param.8) | copy-start | bytes 720004
  5.3 12.3 %collective-permute-start = (bf16[600,4,256]{2,0,1:T(8,128)(2,1)}, bf16[600,4,256]{2,0,1:T(8,128)(2,1)}, u32[]{:S(2)}, u32[]{:S(2)}) collective-permute-start(bf16[600,4,256]{2,0,1:T(8,128)(2,1)} %copy.26), channel_id=1, source_target_pairs={{0,1},{1,2},{2,3},{3,4},{4,5},{5,6},{6,7},{7,8},{8,9},{9,10},{10,1... | collective-permute-start | bytes 3686408 | tf_op jit(solution)/shard_map/ppermute | solution.py:20
  9.9 10.1 %collective-permute-start.1 = (bf16[600,4,256]{2,0,1:T(8,128)(2,1)}, bf16[600,4,256]{2,0,1:T(8,128)(2,1)}, u32[]{:S(2)}, u32[]{:S(2)}) collective-permute-start(bf16[600,4,256]{2,0,1:T(8,128)(2,1)} %copy.27), channel_id=1, source_target_pairs={{1,0},{2,1},{3,2},{4,3},{5,4},{6,5},{7,6},{8,7},{9,8},{10,9},{11,1... | collective-permute-start | bytes 3686408 | tf_op jit(solution)/shard_map/ppermute | solution.py:22
  111.6 29.9 %copy-start.3 = (s32[2,600]{1,0:T(2,128)S(1)}, s32[2,600]{1,0:T(2,128)}, u32[]{:S(2)}) copy-start(s32[2,600]{1,0:T(2,128)} %param.9) | copy-start | bytes 14404
  114.2 73.0 %all-to-all-start = ((bf16[16,600,128]{2,1,0:T(8,128)(2,1)}), bf16[16,600,128]{2,1,0:T(8,128)(2,1)S(1)}, u32[]{:S(2)}, u32[]{:S(2)}) async-start(bf16[16,600,128]{2,1,0:T(8,128)(2,1)} %copy.24), calls=%async_computation | async-start | bytes 4915200 | tf_op jit(solution)/shard_map/all_to_all | solution.py:146
  140.5 1.0 copy-start.6
  140.5 1.0 copy-start.5
  142.1 89.7 %copy-start.4 = (s32[600]{0:T(1024)S(1)}, s32[600]{0:T(1024)}, u32[]{:S(2)}) copy-start(s32[600]{0:T(1024)} %get-tuple-element.4) | copy-start | bytes 7204
  231.8 1.6 copy-start.1
  231.8 1.6 copy-start.2
where the time goes:
time: 245 us
  other arithmetic  101 us (41%)
  waiting for transfers between devices  45 us (18%)
  blocking collectives  40.8 us (17%)
  starting transfers between devices  30.2 us (12%)
  local copies, waits for them, and re-layouts  21.9 us (9%)
  matrix products  3.2 us (1%)
    convert_element_type x1, other arithmetic, column_pass(): return summed.astype(jnp.bfloat16)  46.9 us
    all_to_all x1, waiting for transfers between devices, on_device(): lax.all_to_all(slab_major(filtered, slab_count, slab_cols), 'rows', split...  45 us
    psum x1, blocking collectives, on_device(): ref_series = lax.psum(own_term, 'rows')  40.8 us
    convert_element_type x1, other arithmetic, on_device(): (interferograms.astype(jnp.float32) - lowpass).astype(jnp.bfloat16)  25.9 us
    all_to_all x1, starting transfers between devices, on_device(): lax.all_to_all(slab_major(filtered, slab_count, slab_cols), 'rows', split...  25.6 us
    convert_element_type x1, other arithmetic, on_device(): lowpass = row_pass(smoothed.astype(jnp.float32), kernel_taps, local_rows)  7.57 us
    div x1, other arithmetic, solve_small(): solution[row_at] = element / factor[row_at][row_at]  6.61 us
    convert_element_type x1, other arithmetic, column_pass(): values = images.astype(jnp.float32)  6.6 us
  transfers between devices with their start and end apart: 3, of which 1 were waited for; matrix products, arithmetic and copies ran while one was open for 4% of the time, Pallas kernels for 0%

commit v1 on v0

--- a/solution.py
+++ b/solution.py
@@ -137,31 +137,35 @@
     slab_count = lax.axis_size("rows")
     image_count, local_rows, columns = interferograms.shape
     slab_cols = columns // slab_count
-    extended = padded_2(interferograms, (("rows", 1),), RADIUS)
-    smoothed = column_pass(extended, kernel_taps)
-    smoothed = lax.optimization_barrier(smoothed)
-    lowpass = row_pass(smoothed.astype(jnp.float32), kernel_taps, local_rows)
+    smoothed = lax.optimization_barrier(column_pass(interferograms, kernel_taps))
+    extended = padded_2(smoothed, (("rows", 1),), RADIUS)
+    lowpass = row_pass(extended.astype(jnp.float32), kernel_taps, local_rows)
     filtered = (interferograms.astype(jnp.float32) - lowpass).astype(jnp.bfloat16)
     design = design_of(date_pairs)
-    arrived = lax.all_to_all(
-        slab_major(filtered, slab_count, slab_cols), "rows", split_axis=0, concat_axis=0, tiled=True
-    )
-    slab_values = from_sources(arrived)
-    displacement = jnp.dot(pseudo_inverse, slab_values, preferred_element_type=jnp.float32).astype(
+    values = filtered.reshape(image_count, local_rows * columns)
+    displacement = jnp.dot(pseudo_inverse, values, preferred_element_type=jnp.float32).astype(
         jnp.bfloat16
     )
-    misfit = misfit_of(slab_values, displacement, design)
+    misfit = misfit_of(values, displacement, design)
     ref_index = ref_pixel[0]
     ref_row = ref_index // columns
     ref_col = ref_index % columns
-    owner_slab = ref_col // slab_cols
-    local_pixel = ref_row * slab_cols + ref_col - owner_slab * slab_cols
+    owner = ref_row // local_rows
+    local_pixel = (ref_row - owner * local_rows) * columns + ref_col
     own_series = lax.dynamic_slice_in_dim(displacement, local_pixel, 1, 1)[:, 0]
-    own_term = jnp.where(lax.axis_index("rows") == owner_slab, own_series.astype(jnp.float32), 0.0)
+    own_term = jnp.where(lax.axis_index("rows") == owner, own_series.astype(jnp.float32), 0.0)
     ref_series = lax.psum(own_term, "rows")
-    series = (displacement.astype(jnp.float32) - ref_series[:, None]).astype(jnp.bfloat16)
-    kalman_state = kalman_update(series, misfit, prior_mean[0], prior_precision[0])
-    return (series[None], kalman_state[None], misfit[None])
+    packed = jnp.concatenate([displacement, misfit[None]], axis=0)
+    packed = packed.reshape(DATES + 1, local_rows, columns)
+    arrived = from_sources(
+        lax.all_to_all(
+            slab_major(packed, slab_count, slab_cols), "rows", split_axis=0, concat_axis=0, tiled=True
+        )
+    )
+    slab_disp, slab_misfit = arrived[:DATES], arrived[DATES]
+    series = (slab_disp.astype(jnp.float32) - ref_series[:, None]).astype(jnp.bfloat16)
+    kalman_state = kalman_update(series, slab_misfit, prior_mean[0], prior_precision[0])
+    return (series[None], kalman_state[None], slab_misfit[None])
 
 
 def solution(mesh):

time: 245 us -> 155 us (0.63)
  the two profiles are of different devices: /device:TPU:0 before, /device:TPU:1 now
where the time goes in v1:
time: 155 us; the launch traced here: 154 us
  other arithmetic  61.4 us (40%)
  blocking collectives  38.6 us (25%)
  waiting for transfers between devices  24.8 us (16%)
  starting transfers between devices  13.1 us (8%)
  local copies, waits for them, and re-layouts  9.07 us (6%)
  matrix products  4.2 us (3%)
  between operations  2.24 us (1%)
    psum x1, blocking collectives, on_device(): ref_series = lax.psum(own_term, 'rows')  38.6 us
    convert_element_type x1, other arithmetic, column_pass(): return summed.astype(jnp.bfloat16)  26.9 us
    ppermute x1, waiting for transfers between devices, padded_2(): lax.ppermute(tail, axis, [(i, (i + 1) % count) for i in range(ends)])  24.8 us
    unnamed x2, other arithmetic  10.9 us
    div x1, other arithmetic, solve_small(): solution[row_at] = element / factor[row_at][row_at]  7.53 us
    all_to_all x1, starting transfers between devices, on_device(): lax.all_to_all(slab_major(packed, slab_count, slab_cols), 'rows', split_a...  6.67 us
    div x1, other arithmetic, solve_small(): forward.append(element / factor[row_at][row_at])  5.4 us
    ppermute x1, starting transfers between devices, padded_2(): lax.ppermute(tail, axis, [(i, (i + 1) % count) for i in range(ends)])  4.54 us
  transfers between devices with their start and end apart: 3, of which 1 were waited for; matrix products, arithmetic and copies ran while one was open for 1% of the time, Pallas kernels for 0%

profile of v1, /device:TPU:1, one launch (start us, length us, event | category | flops | bytes accessed | tf_op | source)
XLA Modules:
  0.0 153.5 jit_solution(9260032425087313595)
XLA Ops:
  0.6 0.0 copy-start
  1.3 0.6 fusion.52
  1.9 0.7 broadcast_divide_fusion
  2.6 0.7 fusion.58
  3.3 4.4 %copy_convert_fusion = f32[600,8,256]{2,0,1:T(8,128)} fusion(bf16[600,8,256]{2,1,0:T(8,128)(2,1)} %param.7), kind=kLoop, calls=%fused_computation.47 | loop fusion | flops 1228800 | bytes 7372800 | tf_op jit(solution)/shard_map/convert_element_type | solution.py:143
  7.6 0.0 copy-start.5
  7.7 26.9 %fusion.9 = bf16[600,8,256]{2,0,1:T(8,128)(2,1)S(1)} fusion(f32[600,8,256]{2,0,1:T(8,128)} %copy_convert_fusion, f32[]{:T(128)} %bitcast.9, f32[]{:T(128)} %bitcast.8, f32[]{:T(128)} %bitcast.7, f32[]{:T(128)} %bitcast.6, f32[]{:T(128)} %bitcast.5, f32[]{:T(128)} %bitcast.4, f32[]{:T(128)} %bitcast.3, f32[]{:T(128)} %bitcast.2, f32[]{:T(128)} %bitcast.1), kind=kLoop, calls=%fused_computation.17 | loop fusion | flops 22118400 | bytes 7372836 | tf_op jit(solution)/shard_map/convert_element_type | solution.py:43
  34.5 0.2 fusion.56
  34.7 4.5 %collective-permute-start = (bf16[600,4,256]{2,0,1:T(8,128)(2,1)S(1)}, bf16[600,4,256]{2,0,1:T(8,128)(2,1)S(1)}, u32[]{:S(2)}, u32[]{:S(2)}) collective-permute-start(bf16[600,4,256]{2,0,1:T(8,128)(2,1)S(1)} %get-tuple-element.16), channel_id=1, source_target_pairs={{0,1},{1,2},{2,3},{3,4},{4,5},{5,6},{6,7},{7,8},{8,9},{9,10},{10,1... | collective-permute-start | bytes 3686408 | tf_op jit(solution)/shard_map/ppermute | solution.py:20
  39.3 1.9 %collective-permute-start.1 = (bf16[600,4,256]{2,0,1:T(8,128)(2,1)S(1)}, bf16[600,4,256]{2,0,1:T(8,128)(2,1)}, u32[]{:S(2)}, u32[]{:S(2)}) collective-permute-start(bf16[600,4,256]{2,0,1:T(8,128)(2,1)S(1)} %get-tuple-element.17), channel_id=1, source_target_pairs={{1,0},{2,1},{3,2},{4,3},{5,4},{6,5},{7,6},{8,7},{9,8},{10,9},{11,1... | collective-permute-start | bytes 3686408 | tf_op jit(solution)/shard_map/ppermute | solution.py:22
  41.2 0.0 copy-done.5
  41.2 0.0 copy-start.1
  41.2 24.8 %collective-permute-done = bf16[600,4,256]{2,0,1:T(8,128)(2,1)S(1)} collective-permute-done((bf16[600,4,256]{2,0,1:T(8,128)(2,1)S(1)}, bf16[600,4,256]{2,0,1:T(8,128)(2,1)S(1)}, u32[]{:S(2)}, u32[]{:S(2)}) %collective-permute-start) | collective-permute-done | bytes 1228832 | tf_op jit(solution)/shard_map/ppermute | solution.py:20
  66.1 0.0 collective-permute-done.1
  66.1 1.9 %maximum_convert_fusion = f32[600,16,256]{2,0,1:T(8,128)S(1)} fusion(bf16[600,4,256]{2,0,1:T(8,128)(2,1)} %collective-permute-done.1, bf16[600,8,256]{2,0,1:T(8,128)(2,1)S(1)} %fusion.9, bf16[600,4,256]{2,0,1:T(8,128)(2,1)S(1)} %collective-permute-done), kind=kLoop, calls=%fused_computation.44 | loop fusion | flops 7372800 | bytes 14745600 | tf_op jit(solution)/shard_map/convert_element_type | solution.py:142
  68.0 0.0 copy-done.1
  68.0 10.7 %fusion.27 = bf16[8,75,8,256]{3,2,1,0:T(8,128)(2,1)S(1)} fusion(f32[600,16,256]{2,0,1:T(8,128)S(1)} %maximum_convert_fusion, f32[]{:T(128)} %bitcast.9, f32[]{:T(128)} %bitcast.8, f32[]{:T(128)} %bitcast.7, f32[]{:T(128)} %bitcast.6, f32[]{:T(128)} %bitcast.5, f32[]{:T(128)} %bitcast.4, f32[]{:T(128)} %bitcast.3, f32[]{:T(128)} %bitcast.2, f32[]{:T(128)} %bitcast.1, ...), kind=kLoop, calls=%fused_computation.48 | loop fusion | flops 24576000 | bytes 49152036
  78.8 0.3 copy.31
  79.1 0.0 copy-start.3
  79.1 0.0 copy-done
  79.1 0.8 convolution_convert_fusion
  80.0 0.6 copy-done.3
  80.6 0.0 copy-start.4
  80.6 0.5 copy.25
  81.1 2.6 %multiply_reduce_fusion = f32[2048]{0:T(1024)S(1)} fusion(bf16[600,2048]{1,0:T(8,128)(2,1)} %bitcast.164, bf16[2048,200]{0,1:T(8,128)(2,1)S(1)} %convolution_convert_fusion, s32[600]{0:T(1024)S(1)} %get-tuple-element.4, s32[600]{0:T(1024)S(1)} %get-tuple-element.3), kind=kOutput, calls=%fused_computation.45 | convolution fusion | flops 497153152 | bytes 3289792 | tf_op jit(solution)/shard_map/dot_general | solution.py:69
  83.7 0.0 copy-done.4
  83.7 1.0 convert_element_type.180
  84.8 0.3 maximum_bitcast_fusion
  85.1 0.1 copy.27
  85.2 1.3 copy.28
  86.5 6.7 %all-to-all-start = ((bf16[16,201,128]{2,1,0:T(8,128)(2,1)}), bf16[16,201,128]{2,1,0:T(8,128)(2,1)S(1)}, u32[]{:S(2)}, u32[]{:S(2)}) async-start(bf16[16,201,128]{2,1,0:T(8,128)(2,1)} %copy.28), calls=%async_computation | async-start | bytes 1703936 | tf_op jit(solution)/shard_map/all_to_all | solution.py:161
  93.9 0.1 fusion.49
  93.9 0.1 add_multiply_fusion
  94.0 0.2 fusion.53
  94.2 0.7 fusion.57
  94.9 1.0 select_reduce_fusion
  95.8 38.6 %psum.7 = f32[200]{0:T(256)S(1)} all-reduce(f32[200]{0:T(256)S(1)} %select_reduce_fusion), channel_id=1, replica_groups=mesh['frame'=2,'rows'=16] {'rows'}, use_global_device_ids=true, to_apply=%region_2.3 | all-reduce | flops 200 | bytes 1600 | tf_op jit(solution)/shard_map/psum | solution.py:157
  134.4 0.0 all-to-all-done
  134.4 0.0 copy-start.2
  134.4 0.2 fusion.32
  134.7 0.7 copy-done.2
  135.3 1.5 copy.29
  136.8 1.5 reshape.505
  138.4 0.5 fusion.29
  138.9 1.1 subtract_convert_fusion
  139.9 5.4 %subtract_divide_fusion.3 = (f32[1,2048]{1,0:T(1,128)S(1)}, f32[1,2048]{1,0:T(1,128)S(1)}, f32[1,2048]{1,0:T(1,128)S(1)}, f32[1,2048]{1,0:T(1,128)S(1)}, f32[1,2...) fusion(f32[4,2048]{1,0:T(4,128)S(1)} %fusion.29, f32[1,4,2048]{2,1,0:T(4,128)} %param.12, ...), kind=kLoop, calls=%fused_computation.96 | loop fusion | flops 92160 | bytes 131096 | tf_op jit(solution)/shard_map/div | solution.py:103
  145.3 7.5 %subtract_divide_fusion = (f32[1,2048]{1,0:T(1,128)S(1)}, f32[1,2048]{1,0:T(1,128)S(1)}, f32[1,2048]{1,0:T(1,128)S(1)}, f32[1,2048]{1,0:T(1,128)S(1)}) fusion(f32[1,2048]{1,0:T(1,128)S(1)} %get-tuple-element.11, f32[1,2048]{1,0:T(1,128)S(1)} %get-tuple-element.14, f32[]{:T(128)} %bitcast.25, f32[]{:T(128)} %bitcast.30, f32[]{:T(128)} %bitcast.20, ...), kind=kLoop, calls=%fused_computation.89 | loop fusion | flops 149504 | bytes 131112 | tf_op jit(solution)/shard_map/div | solution.py:109
  152.9 0.7 maximum_bitcast_fusion.1
  (3 shorter events, 0.0 us)
Async XLA Ops:
  0.6 78.5 %copy-start = (bf16[200,600]{1,0:T(8,128)(2,1)S(1)}, bf16[200,600]{1,0:T(8,128)(2,1)}, u32[]{:S(2)}) copy-start(bf16[200,600]{1,0:T(8,128)(2,1)} %param.8) | copy-start | bytes 720004
  7.6 33.5 %copy-start.5 = (s32[2,600]{1,0:T(2,128)S(1)}, s32[2,600]{1,0:T(2,128)}, u32[]{:S(2)}) copy-start(s32[2,600]{1,0:T(2,128)} %param.9) | copy-start | bytes 14404
  34.7 31.4 %collective-permute-start = (bf16[600,4,256]{2,0,1:T(8,128)(2,1)S(1)}, bf16[600,4,256]{2,0,1:T(8,128)(2,1)S(1)}, u32[]{:S(2)}, u32[]{:S(2)}) collective-permute-start(bf16[600,4,256]{2,0,1:T(8,128)(2,1)S(1)} %get-tuple-element.16), channel_id=1, source_target_pairs={{0,1},{1,2},{2,3},{3,4},{4,5},{5,6},{6,7},{7,8},{8,9},{9,10},{10,1... | collective-permute-start | bytes 3686408 | tf_op jit(solution)/shard_map/ppermute | solution.py:20
  39.3 26.8 %collective-permute-start.1 = (bf16[600,4,256]{2,0,1:T(8,128)(2,1)S(1)}, bf16[600,4,256]{2,0,1:T(8,128)(2,1)}, u32[]{:S(2)}, u32[]{:S(2)}) collective-permute-start(bf16[600,4,256]{2,0,1:T(8,128)(2,1)S(1)} %get-tuple-element.17), channel_id=1, source_target_pairs={{1,0},{2,1},{3,2},{4,3},{5,4},{6,5},{7,6},{8,7},{9,8},{10,9},{11,1... | collective-permute-start | bytes 3686408 | tf_op jit(solution)/shard_map/ppermute | solution.py:22
  41.2 26.8 %copy-start.1 = (bf16[600,8,256]{2,1,0:T(8,128)(2,1)S(1)}, bf16[600,8,256]{2,1,0:T(8,128)(2,1)}, u32[]{:S(2)}) copy-start(bf16[600,8,256]{2,1,0:T(8,128)(2,1)} %param.7) | copy-start | bytes 7372804
  79.1 1.4 copy-start.3
  80.6 3.2 %copy-start.4 = (bf16[2048,200]{0,1:T(8,128)(2,1)}, bf16[2048,200]{0,1:T(8,128)(2,1)S(1)}, u32[]{:S(2)}) copy-start(bf16[2048,200]{0,1:T(8,128)(2,1)S(1)} %convolution_convert_fusion) | copy-start | bytes 2457604
  86.5 48.0 %all-to-all-start = ((bf16[16,201,128]{2,1,0:T(8,128)(2,1)}), bf16[16,201,128]{2,1,0:T(8,128)(2,1)S(1)}, u32[]{:S(2)}, u32[]{:S(2)}) async-start(bf16[16,201,128]{2,1,0:T(8,128)(2,1)} %copy.28), calls=%async_computation | async-start | bytes 1703936 | tf_op jit(solution)/shard_map/all_to_all | solution.py:161
  134.4 0.9 copy-start.2

commit v2 on v1

--- a/solution.py
+++ b/solution.py
@@ -1,12 +1,18 @@
+import functools
 import math
 
 import jax
 import jax.numpy as jnp
+import ml_dtypes
+import numpy as np
 from jax import lax
+from jax.experimental import pallas as pl
+from jax.experimental.pallas import tpu as pltpu
 from jax.sharding import PartitionSpec as P
 
 DATES = 200
 RADIUS = 4
+MESH = pl.DeviceIdType.MESH
 
 
 def padded_2(cells, sides, width):
@@ -130,7 +136,7 @@
     return jnp.stack(solve_small(matrix, right_side), axis=0)
 
 
-def on_device(
+def in_steps(
     interferograms, pseudo_inverse, date_pairs, ref_pixel, band_width, prior_mean, prior_precision
 ):
     kernel_taps = filter_taps(band_width)
@@ -168,6 +174,449 @@
     return (series[None], kalman_state[None], slab_misfit[None])
 
 
+PAD_IMAGES = 608
+PAD_DEPTH = 640
+PAD_DATES = 208
+LANES = 128
+HALVES = 2
+RAISED = 56 * 1024 * 1024
+
+
+def split_three(values):
+    first = values.astype(jnp.bfloat16)
+    rest = values - first.astype(jnp.float32)
+    second = rest.astype(jnp.bfloat16)
+    third = (rest - second.astype(jnp.float32)).astype(jnp.bfloat16)
+    return first, second, third
+
+
+def dot_f32(left, right):
+    return jnp.dot(left, right, preferred_element_type=jnp.float32)
+
+
+def iota(shape, dim):
+    return lax.broadcasted_iota(jnp.int32, shape, dim)
+
+
+def column_of(lane, half, slab_cols):
+    return (HALVES * (lane // slab_cols) + half) * slab_cols + lane % slab_cols
+
+
+def kernel(
+    n,
+    gram,
+    ifg_ref,
+    pinv_ref,
+    pairs_ref,
+    pixel_ref,
+    band_ref,
+    mean_ref,
+    precision_ref,
+    trend_ref,
+    series_ref,
+    state_ref,
+    misfit_ref,
+    by_row,
+    weights,
+    own,
+    smooth,
+    halo,
+    filt,
+    pinv_s,
+    design_s,
+    disp_s,
+    sent,
+    recv,
+    ref_out,
+    ref_in,
+    proj,
+    halo_send,
+    halo_recv,
+    part_send,
+    part_recv,
+    ref_send,
+    ref_recv,
+    self_sem,
+):
+    images, local_rows, columns = ifg_ref.shape
+    slab_cols = columns // n
+    per_half = n // HALVES
+    me = lax.axis_index("rows")
+
+    barrier = pltpu.get_barrier_semaphore()
+
+    @pl.loop(1, n)
+    def _(k):
+        pl.semaphore_signal(barrier, inc=1, device_id={"rows": lax.rem(me + k, n)}, device_id_type=MESH)
+
+    spread = jnp.full((8, LANES), band_ref[0], jnp.int32).astype(jnp.float32) / 10.0
+    denominator = 2.0 * spread * spread
+    raw = [jnp.exp(jnp.full((8, LANES), -float(k * k), jnp.float32) / denominator) for k in range(RADIUS + 1)]
+    total = raw[0]
+    for k in range(1, RADIUS + 1):
+        total = total + 2.0 * raw[k]
+    taps = [value / total for value in raw]
+    lane = iota((columns, columns), 1)
+    source = column_of(lane % LANES, lane // LANES, slab_cols)
+    away = jnp.abs(iota((columns, columns), 0) - source)
+    banded = jnp.zeros((columns, columns), jnp.float32)
+    for k in range(RADIUS + 1):
+        banded = jnp.where(away == k, taps[k][0:1, 0:1], banded)
+    for at, piece in enumerate(split_three(banded)):
+        weights[at] = piece
+    weights[3] = jnp.where(away == 0, 1.0, 0.0).astype(jnp.bfloat16)
+
+    size = 16 * local_rows
+    out_at, in_at = iota((size, size), 0), iota((size, size), 1)
+    order = jnp.where((out_at % 16) * local_rows + out_at // 16 == in_at, 1.0, 0.0).astype(jnp.bfloat16)
+
+    def regroup(values, first):
+        moved = dot_f32(order, values.astype(jnp.bfloat16)).astype(jnp.bfloat16)
+        for r in range(local_rows):
+            by_row[r, pl.ds(first, 16), :] = moved[r * 16 : (r + 1) * 16]
+
+    whole = images // 16
+
+    @pl.loop(0, whole, unroll=True)
+    def _(g):
+        first = pl.multiple_of(g * 16, 16)
+        values = ifg_ref[pl.ds(first, 16)].astype(jnp.float32)
+        regroup(values.reshape(size, columns), first)
+
+    left_over = images - whole * 16
+    if left_over:
+        values = ifg_ref[whole * 16 :].astype(jnp.float32).reshape(left_over * local_rows, columns)
+        regroup(
+            jnp.concatenate([values, jnp.zeros((size - left_over * local_rows, columns), jnp.float32)], axis=0),
+            whole * 16,
+        )
+
+    def smooth_row(r):
+        values = by_row[r]
+        made = dot_f32(values, weights[0]) + dot_f32(values, weights[1]) + dot_f32(values, weights[2])
+        made = made.astype(jnp.bfloat16)
+        for h in range(HALVES):
+            smooth[h, r] = made[:, h * LANES : (h + 1) * LANES]
+
+    def halo_copy(down, h):
+        rows = pl.ds(local_rows - RADIUS, RADIUS) if down else pl.ds(0, RADIUS)
+        side = 0 if down else 1
+        to = jnp.minimum(me + 1, n - 1) if down else jnp.maximum(me - 1, 0)
+        return pltpu.make_async_remote_copy(
+            src_ref=smooth.at[h, rows],
+            dst_ref=halo.at[side, h],
+            send_sem=halo_send.at[side, h],
+            recv_sem=halo_recv.at[side, h],
+            device_id={"rows": to},
+            device_id_type=MESH,
+        )
+
+    pl.loop(local_rows - RADIUS, local_rows)(smooth_row)
+    pl.semaphore_wait(barrier, n - 1)
+
+    @pl.when(me < n - 1)
+    def _():
+        halo_copy(True, 0).start()
+
+    pl.loop(0, local_rows - RADIUS)(smooth_row)
+
+    @pl.when(me > 0)
+    def _():
+        halo_copy(False, 0).start()
+
+    @pl.when(me < n - 1)
+    def _():
+        halo_copy(True, 1).start()
+
+    @pl.when(me > 0)
+    def _():
+        halo_copy(False, 1).start()
+
+    @pl.loop(0, local_rows)
+    def _(r):
+        made = dot_f32(by_row[r], weights[3]).astype(jnp.bfloat16)
+        for h in range(HALVES):
+            own[h, r] = made[:, h * LANES : (h + 1) * LANES]
+
+    @pl.when(me == 0)
+    def _():
+        halo[0] = jnp.zeros(halo.shape[1:], halo.dtype)
+
+    @pl.when(me == n - 1)
+    def _():
+        halo[1] = jnp.zeros(halo.shape[1:], halo.dtype)
+
+    pinv_s[...] = jnp.zeros_like(pinv_s)
+    pinv_s[0:DATES, 0:images] = pinv_ref[...]
+    date = iota((256, images), 0)
+    later = jnp.where(date == pairs_ref[1:2, :], 1.0, 0.0)
+    earlier = jnp.where(date == pairs_ref[0:1, :], 1.0, 0.0)
+    both = jnp.concatenate([later - earlier, jnp.zeros((256, PAD_DEPTH - images), jnp.float32)], axis=1)
+    design_s[...] = both.T.astype(jnp.bfloat16)
+    filt[PAD_IMAGES:, :] = jnp.zeros((PAD_DEPTH - PAD_IMAGES, local_rows * LANES), jnp.bfloat16)
+
+    pixel = pixel_ref[0]
+    ref_row, ref_col = pixel // columns, pixel % columns
+    ref_total = jnp.zeros((16, 256), jnp.float32)
+    block_lanes = 256
+
+    def part_copy(h, k):
+        q = lax.rem(me // HALVES + k, per_half)
+        return pltpu.make_async_remote_copy(
+            src_ref=sent.at[h, q],
+            dst_ref=recv.at[me],
+            send_sem=part_send.at[h, k],
+            recv_sem=part_recv.at[me],
+            device_id={"rows": HALVES * q + h},
+            device_id_type=MESH,
+        )
+
+    def ref_copy(k):
+        return pltpu.make_async_remote_copy(
+            src_ref=ref_out,
+            dst_ref=ref_in.at[me],
+            send_sem=ref_send.at[k],
+            recv_sem=ref_recv.at[me],
+            device_id={"rows": lax.rem(me + k, n)},
+            device_id_type=MESH,
+        )
+
+    for h in range(HALVES):
+
+        @pl.when(me > 0)
+        def _():
+            halo_copy(True, h).wait_recv()
+
+        @pl.when(me < n - 1)
+        def _():
+            halo_copy(False, h).wait_recv()
+
+        @pl.loop(0, PAD_IMAGES // 16)
+        def _(g):
+            block = pl.ds(pl.multiple_of(g * 16, 16), 16)
+            lines = [halo[0, h, t, block, :] for t in range(RADIUS)]
+            lines += [smooth[h, r, block, :] for r in range(local_rows)]
+            lines += [halo[1, h, t, block, :] for t in range(RADIUS)]
+            lines = [line.astype(jnp.float32) for line in lines]
+            for r in range(local_rows):
+                low = lines[r + RADIUS] * taps[0][0:1]
+                for k in range(1, RADIUS + 1):
+                    low = low + (lines[r + RADIUS - k] + lines[r + RADIUS + k]) * taps[k][0:1]
+                high = own[h, r, block, :].astype(jnp.float32) - low
+                filt[block, r * LANES : (r + 1) * LANES] = high.astype(jnp.bfloat16)
+
+        for b in range(local_rows * LANES // block_lanes):
+            lanes = slice(b * block_lanes, (b + 1) * block_lanes)
+            values = filt[:, lanes]
+            disp = dot_f32(pinv_s[...], values).astype(jnp.bfloat16)
+            disp_wide = jnp.concatenate([disp, jnp.zeros((256 - PAD_DATES, block_lanes), jnp.bfloat16)], axis=0)
+            residual = values.astype(jnp.float32) - dot_f32(design_s[...], disp_wide)
+            misfit = jnp.sum(residual * residual, axis=0, keepdims=True) / images
+            at = iota((16, block_lanes), 1) + b * block_lanes
+            hit = (at // LANES + me * local_rows == ref_row) & (column_of(at % LANES, h, slab_cols) == ref_col)
+            ref_total += lax.dot_general(
+                jnp.where(hit, 1.0, 0.0).astype(jnp.bfloat16),
+                disp_wide,
+                (((1,), (1,)), ((), ())),
+                preferred_element_type=jnp.float32,
+            )
+            disp_s[0:DATES, lanes] = disp[0:DATES].astype(jnp.float32)
+            disp_s[DATES:, lanes] = jnp.broadcast_to(misfit, (PAD_DATES - DATES, block_lanes))
+
+        if h == HALVES - 1:
+            ref_out[...] = ref_total.astype(jnp.bfloat16)
+
+            @pl.loop(1, n)
+            def _(k):
+                ref_copy(k).start()
+
+        @pl.loop(0, PAD_DATES // 16)
+        def _(g):
+            block = pl.ds(pl.multiple_of(g * 16, 16), 16)
+            lines = [disp_s[block, r * LANES : (r + 1) * LANES] for r in range(local_rows)]
+            place = iota((16, LANES), 1) // slab_cols
+            for q in range(per_half):
+                made = None
+                for r in range(local_rows):
+                    shift = ((r - q) * slab_cols) % LANES
+                    moved = pltpu.roll(lines[r], shift, 1) if shift else lines[r]
+                    made = moved if made is None else jnp.where(place == r, moved, made)
+                sent[h, q, block, :] = made.astype(jnp.bfloat16)
+
+        @pl.when(me % HALVES == h)
+        def _():
+            local = pltpu.make_async_copy(sent.at[h, me // HALVES], recv.at[me], self_sem)
+            local.start()
+            local.wait()
+
+        @pl.when(me % HALVES != h)
+        def _():
+            part_copy(h, 0).start()
+
+        @pl.loop(1, per_half)
+        def _(k):
+            part_copy(h, k).start()
+
+    @pl.loop(1, n)
+    def _(k):
+        j = lax.rem(me + k, n)
+        pltpu.make_async_remote_copy(
+            src_ref=ref_out,
+            dst_ref=ref_in.at[j],
+            send_sem=ref_send.at[k],
+            recv_sem=ref_recv.at[j],
+            device_id={"rows": j},
+            device_id_type=MESH,
+        ).wait_recv()
+
+    ref_in[me] = ref_out[...]
+    ref_sum = ref_in[0].astype(jnp.float32)
+    for j in range(1, n):
+        ref_sum = ref_sum + ref_in[j].astype(jnp.float32)
+    ref_column = jnp.broadcast_to(ref_sum[0:1], (LANES, 256)).T[0:PAD_DATES]
+
+    @pl.loop(0, n)
+    def _(k):
+        j = lax.rem(me + k, n)
+
+        @pl.when(k > 0)
+        def _():
+            pltpu.make_async_remote_copy(
+                src_ref=sent.at[0, 0],
+                dst_ref=recv.at[j],
+                send_sem=part_send.at[0, 0],
+                recv_sem=part_recv.at[j],
+                device_id={"rows": j},
+                device_id_type=MESH,
+            ).wait_recv()
+
+        values = recv[j].astype(jnp.float32)
+        lanes = pl.ds(pl.multiple_of(j * LANES, LANES), LANES)
+        series = (values - ref_column).astype(jnp.bfloat16)
+        series_ref[0, :, lanes] = series[0:DATES]
+        made = dot_f32(trend_ref[...], series)
+        proj[0:4, lanes] = made[0:4] + (made[4:8] + made[8:12])
+        proj[4:5, lanes] = values[DATES : DATES + 1]
+
+    misfit = proj[4:5, :]
+    misfit_ref[...] = misfit.astype(jnp.bfloat16)
+    inverse_noise = 1.0 / (0.1 + misfit)
+    precision = [precision_ref[0, d : d + 1, :] for d in range(4)]
+    matrix = [
+        [float(gram[a][b]) * inverse_noise + (precision[a] if a == b else 0.0) for b in range(4)]
+        for a in range(4)
+    ]
+    right_side = [precision[d] * mean_ref[0, d : d + 1, :] + proj[d : d + 1, :] * inverse_noise for d in range(4)]
+    for d, value in enumerate(solve_small(matrix, right_side)):
+        state_ref[0, d : d + 1, :] = value
+
+    for h in range(HALVES):
+
+        @pl.when(me < n - 1)
+        def _():
+            halo_copy(True, h).wait_send()
+
+        @pl.when(me > 0)
+        def _():
+            halo_copy(False, h).wait_send()
+
+        @pl.when(me % HALVES != h)
+        def _():
+            part_copy(h, 0).wait_send()
+
+        @pl.loop(1, per_half)
+        def _(k):
+            part_copy(h, k).wait_send()
+
+    @pl.loop(1, n)
+    def _(k):
+        ref_copy(k).wait_send()
+
+
+def trend_constants():
+    epochs = np.arange(DATES, dtype=np.float64)
+    phase = 2.0 * np.pi * 12.0 / 365.25 * epochs
+    rows = np.stack([np.ones_like(epochs), (epochs - (DATES - 1) / 2.0) / DATES, np.cos(phase), np.sin(phase)])
+    return rows.astype(np.float32)
+
+
+def in_kernel(interferograms, pseudo_inverse, date_pairs, ref_pixel, band_width, prior_mean, prior_precision):
+    n = lax.axis_size("rows")
+    images, local_rows, columns = interferograms.shape
+    rows = trend_constants()
+    gram = (rows.astype(np.float64) @ rows.astype(np.float64).T).astype(np.float32)
+    pieces, rest = [], rows
+    for _ in range(3):
+        piece = rest.astype(ml_dtypes.bfloat16)
+        pieces.append(piece)
+        rest = rest - piece.astype(np.float32)
+    trend = np.zeros((16, PAD_DATES), ml_dtypes.bfloat16)
+    trend[0:12, 0:DATES] = np.concatenate(pieces, axis=0)
+    vmem, smem = pl.BlockSpec(memory_space=pltpu.VMEM), pl.BlockSpec(memory_space=pltpu.SMEM)
+    half_rows = (HALVES, local_rows, PAD_IMAGES, LANES)
+    bf16, f32 = jnp.bfloat16, jnp.float32
+    per_half = n // HALVES
+    dma = pltpu.SemaphoreType.DMA
+    return pl.pallas_call(
+        functools.partial(kernel, n, gram.tolist()),
+        out_shape=(
+            jax.ShapeDtypeStruct((1, DATES, n * LANES), bf16),
+            jax.ShapeDtypeStruct((1, 4, n * LANES), f32),
+            jax.ShapeDtypeStruct((1, n * LANES), bf16),
+        ),
+        in_specs=[vmem, vmem, vmem, smem, smem, vmem, vmem, vmem],
+        out_specs=(vmem, vmem, vmem),
+        scratch_shapes=[
+            pltpu.VMEM((local_rows, PAD_IMAGES, columns), bf16),
+            pltpu.VMEM((4, columns, columns), bf16),
+            pltpu.VMEM(half_rows, bf16),
+            pltpu.VMEM(half_rows, bf16),
+            pltpu.VMEM((2, HALVES, RADIUS, PAD_IMAGES, LANES), bf16),
+            pltpu.VMEM((PAD_DEPTH, local_rows * LANES), bf16),
+            pltpu.VMEM((PAD_DATES, PAD_DEPTH), bf16),
+            pltpu.VMEM((PAD_DEPTH, 256), bf16),
+            pltpu.VMEM((PAD_DATES, local_rows * LANES), f32),
+            pltpu.VMEM((HALVES, per_half, PAD_DATES, LANES), bf16),
+            pltpu.VMEM((n, PAD_DATES, LANES), bf16),
+            pltpu.VMEM((16, 256), bf16),
+            pltpu.VMEM((n, 16, 256), bf16),
+            pltpu.VMEM((8, n * LANES), f32),
+            dma((2, HALVES)),
+            dma((2, HALVES)),
+            dma((HALVES, per_half)),
+            dma((n,)),
+            dma((n,)),
+            dma((n,)),
+            dma,
+        ],
+        compiler_params=pltpu.CompilerParams(
+            collective_id=0, has_side_effects=True, vmem_limit_bytes=RAISED
+        ),
+    )(
+        interferograms,
+        pseudo_inverse,
+        date_pairs,
+        ref_pixel,
+        band_width,
+        prior_mean,
+        prior_precision,
+        jnp.asarray(trend),
+    )
+
+
+def on_device(
+    interferograms, pseudo_inverse, date_pairs, ref_pixel, band_width, prior_mean, prior_precision
+):
+    n = lax.axis_size("rows")
+    images, local_rows, columns = interferograms.shape
+    fits = (columns // n) * local_rows == LANES and columns == HALVES * LANES and n % HALVES == 0
+    fits = fits and local_rows == 2 * RADIUS and images == 600
+    chosen = in_kernel if fits else in_steps
+    return chosen(
+        interferograms, pseudo_inverse, date_pairs, ref_pixel, band_width, prior_mean, prior_precision
+    )
+
+
 def solution(mesh):
     placed = (
         P(None, ("frame", "rows"), None),

time: 155 us -> 63.2 us (0.41)
  other arithmetic: 61.4 us -> 0 us
  Pallas kernels: 0 us -> 55.7 us
  blocking collectives: 38.6 us -> 0 us
  waiting for transfers between devices: 24.8 us -> 0 us
  starting transfers between devices: 13.1 us -> 0 us
  local copies, waits for them, and re-layouts: 9.07 us -> 4.79 us
  matrix products: 4.2 us -> 0 us
    pallas_call x0 -> x1, Pallas kernels: none -> 55.7 us  [in_kernel(): pl.pallas_call(functools.partial(kernel, n, gram.tolist()), out_shape=(ja...]
    psum x1 -> x0, blocking collectives: 38.6 us -> none  [on_device(): ref_series = lax.psum(own_term, 'rows')]
    convert_element_type x5 -> x0, other arithmetic: 34.2 us -> none  [the longest x1 26.9 us: column_pass(): return summed.astype(jnp.bfloat16)]
    ppermute x2 -> x0, waiting for transfers between devices: 24.8 us -> none  [the longest x1 24.8 us: padded_2(): lax.ppermute(tail, axis, [(i, (i + 1) % count) for i in range(ends)])]
    div x4 -> x0, other arithmetic: 13.6 us -> none  [the longest x1 7.53 us: solve_small(): solution[row_at] = element / factor[row_at][row_at]]
    unnamed x2 -> x0, other arithmetic: 10.9 us -> none
    all_to_all x1 -> x0, starting transfers between devices: 6.67 us -> none  [on_device(): lax.all_to_all(slab_major(packed, slab_count, slab_cols), 'rows', split_a...]
    ppermute x2 -> x0, starting transfers between devices: 6.46 us -> none  [the longest x1 4.54 us: padded_2(): lax.ppermute(tail, axis, [(i, (i + 1) % count) for i in range(ends)])]
  transfers between devices with their start and end apart: 3 -> 0, of which waited for: 1 -> 0; matrix products, arithmetic and copies ran while one was open for 1% -> 0% of each run, Pallas kernels for 0% -> 0%
where the time goes in v2:
time: 63.2 us; the launch traced here: 62.4 us
  Pallas kernels  55.7 us (88%)
  local copies, waits for them, and re-layouts  4.79 us (8%)
  between operations  1.93 us (3%)
    pallas_call x1, Pallas kernels, in_kernel(): pl.pallas_call(functools.partial(kernel, n, gram.tolist()), out_shape=(ja...  55.7 us
    unnamed x3, local copies, waits for them, and re-layouts  4.79 us

profile of v2, /device:TPU:1, one launch (start us, length us, event | category | flops | bytes accessed | tf_op | source)
XLA Modules:
  0.0 62.4 jit_solution(14219105459287688021)
XLA Ops:
  1.9 55.7 %shard_map.103 = (bf16[1,200,2048]{2,1,0:T(8,128)(2,1)}, f32[1,4,2048]{2,1,0:T(4,128)}, bf16[1,2048]{1,0:T(2,128)(2,1)}) custom-call(bf16[600,8,256]{2,1,0:T(8,128)(2,1)} %ifg_ref.1, bf16[200,600]{1,0:T(8,128)(2,1)} %pinv_ref.1, s32[2,600]{1,0:T(2,128)} %pairs_ref.1, s32[1]{0:T(128)S(6)} %copy.14.pixel_ref, s32[1]{0:T(128)S(6)} %copy.15.band_ref, ...), custom_call_target="tpu_custom_call" | custom-call | tf_op jit(solution)/shard_map/pallas_call | solution.py:560
  57.6 2.1 %copy.16 = bf16[1,200,2048]{2,1,0:T(8,128)(2,1)} copy(bf16[1,200,2048]{2,1,0:T(8,128)(2,1)} %get-tuple-element.6) | data formatting | bytes 1638400
  59.8 1.4 %copy.17 = f32[1,4,2048]{2,1,0:T(4,128)} copy(f32[1,4,2048]{2,1,0:T(4,128)} %get-tuple-element.7) | data formatting | bytes 65536
  61.1 1.3 %copy.18 = bf16[1,2048]{1,0:T(2,128)(2,1)} copy(bf16[1,2048]{1,0:T(2,128)(2,1)} %get-tuple-element.8) | data formatting | bytes 8192

commit v3 on v2

--- a/solution.py
+++ b/solution.py
@@ -178,6 +178,8 @@
 PAD_DEPTH = 640
 PAD_DATES = 208
 LANES = 128
+GROUP = 32
+UNROLL = True
 HALVES = 2
 RAISED = 56 * 1024 * 1024
 
@@ -204,18 +206,13 @@
 
 def kernel(
     n,
-    gram,
     ifg_ref,
     pinv_ref,
     pairs_ref,
     pixel_ref,
     band_ref,
-    mean_ref,
-    precision_ref,
-    trend_ref,
-    series_ref,
-    state_ref,
-    misfit_ref,
+    recv,
+    ref_sum,
     by_row,
     weights,
     own,
@@ -226,10 +223,9 @@
     design_s,
     disp_s,
     sent,
-    recv,
     ref_out,
     ref_in,
-    proj,
+    round_sem,
     halo_send,
     halo_recv,
     part_send,
@@ -238,16 +234,21 @@
     ref_recv,
     self_sem,
 ):
-    images, local_rows, columns = ifg_ref.shape
+    local_rows, columns = filt.shape[1] // LANES, ifg_ref.shape[1]
+    images = ifg_ref.shape[0] // local_rows
     slab_cols = columns // n
     per_half = n // HALVES
     me = lax.axis_index("rows")
 
     barrier = pltpu.get_barrier_semaphore()
 
-    @pl.loop(1, n)
-    def _(k):
-        pl.semaphore_signal(barrier, inc=1, device_id={"rows": lax.rem(me + k, n)}, device_id_type=MESH)
+    partners = [lax.rem(me + away, n) for away in (1, n - 1, 4, n - 4)]
+
+    def greet(semaphore):
+        for partner in partners:
+            pl.semaphore_signal(semaphore, inc=1, device_id={"rows": partner}, device_id_type=MESH)
+
+    greet(barrier)
 
     spread = jnp.full((8, LANES), band_ref[0], jnp.int32).astype(jnp.float32) / 10.0
     denominator = 2.0 * spread * spread
@@ -266,29 +267,27 @@
         weights[at] = piece
     weights[3] = jnp.where(away == 0, 1.0, 0.0).astype(jnp.bfloat16)
 
-    size = 16 * local_rows
+    size = GROUP * local_rows
     out_at, in_at = iota((size, size), 0), iota((size, size), 1)
-    order = jnp.where((out_at % 16) * local_rows + out_at // 16 == in_at, 1.0, 0.0).astype(jnp.bfloat16)
+    order = jnp.where((out_at % GROUP) * local_rows + out_at // GROUP == in_at, 1.0, 0.0).astype(jnp.bfloat16)
 
     def regroup(values, first):
-        moved = dot_f32(order, values.astype(jnp.bfloat16)).astype(jnp.bfloat16)
+        moved = dot_f32(order, values).astype(jnp.bfloat16)
         for r in range(local_rows):
-            by_row[r, pl.ds(first, 16), :] = moved[r * 16 : (r + 1) * 16]
-
-    whole = images // 16
-
-    @pl.loop(0, whole, unroll=True)
+            by_row[r, pl.ds(first, GROUP), :] = moved[r * GROUP : (r + 1) * GROUP]
+
+    whole = images // GROUP
+
+    @pl.loop(0, whole, unroll=UNROLL)
     def _(g):
-        first = pl.multiple_of(g * 16, 16)
-        values = ifg_ref[pl.ds(first, 16)].astype(jnp.float32)
-        regroup(values.reshape(size, columns), first)
-
-    left_over = images - whole * 16
+        regroup(ifg_ref[pl.ds(pl.multiple_of(g * size, size), size), :], pl.multiple_of(g * GROUP, GROUP))
+
+    left_over = images * local_rows - whole * size
     if left_over:
-        values = ifg_ref[whole * 16 :].astype(jnp.float32).reshape(left_over * local_rows, columns)
+        values = ifg_ref[whole * size :, :]
         regroup(
-            jnp.concatenate([values, jnp.zeros((size - left_over * local_rows, columns), jnp.float32)], axis=0),
-            whole * 16,
+            jnp.concatenate([values, jnp.zeros((size - left_over, columns), jnp.bfloat16)], axis=0),
+            whole * GROUP,
         )
 
     def smooth_row(r):
@@ -312,7 +311,7 @@
         )
 
     pl.loop(local_rows - RADIUS, local_rows)(smooth_row)
-    pl.semaphore_wait(barrier, n - 1)
+    pl.semaphore_wait(barrier, len(partners))
 
     @pl.when(me < n - 1)
     def _():
@@ -331,6 +330,8 @@
     @pl.when(me > 0)
     def _():
         halo_copy(False, 1).start()
+
+    greet(round_sem.at[0])
 
     @pl.loop(0, local_rows)
     def _(r):
@@ -345,6 +346,9 @@
     @pl.when(me == n - 1)
     def _():
         halo[1] = jnp.zeros(halo.shape[1:], halo.dtype)
+
+    pl.semaphore_wait(round_sem.at[0], len(partners))
+    greet(round_sem.at[1])
 
     pinv_s[...] = jnp.zeros_like(pinv_s)
     pinv_s[0:DATES, 0:images] = pinv_ref[...]
@@ -355,6 +359,7 @@
     design_s[...] = both.T.astype(jnp.bfloat16)
     filt[PAD_IMAGES:, :] = jnp.zeros((PAD_DEPTH - PAD_IMAGES, local_rows * LANES), jnp.bfloat16)
 
+    pl.semaphore_wait(round_sem.at[1], len(partners))
     pixel = pixel_ref[0]
     ref_row, ref_col = pixel // columns, pixel % columns
     ref_total = jnp.zeros((16, 256), jnp.float32)
@@ -470,28 +475,51 @@
         ).wait_recv()
 
     ref_in[me] = ref_out[...]
-    ref_sum = ref_in[0].astype(jnp.float32)
+    total = ref_in[0].astype(jnp.float32)
     for j in range(1, n):
-        ref_sum = ref_sum + ref_in[j].astype(jnp.float32)
-    ref_column = jnp.broadcast_to(ref_sum[0:1], (LANES, 256)).T[0:PAD_DATES]
-
-    @pl.loop(0, n)
+        total = total + ref_in[j].astype(jnp.float32)
+    ref_sum[...] = total
+
+    @pl.loop(1, n)
     def _(k):
         j = lax.rem(me + k, n)
-
-        @pl.when(k > 0)
+        pltpu.make_async_remote_copy(
+            src_ref=sent.at[0, 0],
+            dst_ref=recv.at[j],
+            send_sem=part_send.at[0, 0],
+            recv_sem=part_recv.at[j],
+            device_id={"rows": j},
+            device_id_type=MESH,
+        ).wait_recv()
+
+    for h in range(HALVES):
+
+        @pl.when(me < n - 1)
         def _():
-            pltpu.make_async_remote_copy(
-                src_ref=sent.at[0, 0],
-                dst_ref=recv.at[j],
-                send_sem=part_send.at[0, 0],
-                recv_sem=part_recv.at[j],
-                device_id={"rows": j},
-                device_id_type=MESH,
-            ).wait_recv()
-
-        values = recv[j].astype(jnp.float32)
-        lanes = pl.ds(pl.multiple_of(j * LANES, LANES), LANES)
+            halo_copy(True, h).wait_send()
+
+        @pl.when(me > 0)
+        def _():
+            halo_copy(False, h).wait_send()
+
+        @pl.when(me % HALVES != h)
+        def _():
+            part_copy(h, 0).wait_send()
+
+        @pl.loop(1, per_half)
+        def _(k):
+            part_copy(h, k).wait_send()
+
+    @pl.loop(1, n)
+    def _(k):
+        ref_copy(k).wait_send()
+
+
+def finish(n, gram, arrived, ref_sum, mean_ref, precision_ref, trend_ref, series_ref, state_ref, misfit_ref, proj):
+    ref_column = jnp.broadcast_to(ref_sum[0:1], (LANES, 256)).T[0:PAD_DATES]
+    for j in range(n):
+        values = arrived[j].astype(jnp.float32)
+        lanes = slice(j * LANES, (j + 1) * LANES)
         series = (values - ref_column).astype(jnp.bfloat16)
         series_ref[0, :, lanes] = series[0:DATES]
         made = dot_f32(trend_ref[...], series)
@@ -509,28 +537,6 @@
     right_side = [precision[d] * mean_ref[0, d : d + 1, :] + proj[d : d + 1, :] * inverse_noise for d in range(4)]
     for d, value in enumerate(solve_small(matrix, right_side)):
         state_ref[0, d : d + 1, :] = value
-
-    for h in range(HALVES):
-
-        @pl.when(me < n - 1)
-        def _():
-            halo_copy(True, h).wait_send()
-
-        @pl.when(me > 0)
-        def _():
-            halo_copy(False, h).wait_send()
-
-        @pl.when(me % HALVES != h)
-        def _():
-            part_copy(h, 0).wait_send()
-
-        @pl.loop(1, per_half)
-        def _(k):
-            part_copy(h, k).wait_send()
-
-    @pl.loop(1, n)
-    def _(k):
-        ref_copy(k).wait_send()
 
 
 def trend_constants():
@@ -557,15 +563,14 @@
     bf16, f32 = jnp.bfloat16, jnp.float32
     per_half = n // HALVES
     dma = pltpu.SemaphoreType.DMA
-    return pl.pallas_call(
-        functools.partial(kernel, n, gram.tolist()),
+    arrived, ref_sum = pl.pallas_call(
+        functools.partial(kernel, n),
         out_shape=(
-            jax.ShapeDtypeStruct((1, DATES, n * LANES), bf16),
-            jax.ShapeDtypeStruct((1, 4, n * LANES), f32),
-            jax.ShapeDtypeStruct((1, n * LANES), bf16),
+            jax.ShapeDtypeStruct((n, PAD_DATES, LANES), bf16),
+            jax.ShapeDtypeStruct((16, 256), f32),
         ),
-        in_specs=[vmem, vmem, vmem, smem, smem, vmem, vmem, vmem],
-        out_specs=(vmem, vmem, vmem),
+        in_specs=[vmem, vmem, vmem, smem, smem],
+        out_specs=(pl.BlockSpec(memory_space=pl.ANY), vmem),
         scratch_shapes=[
             pltpu.VMEM((local_rows, PAD_IMAGES, columns), bf16),
             pltpu.VMEM((4, columns, columns), bf16),
@@ -577,10 +582,9 @@
             pltpu.VMEM((PAD_DEPTH, 256), bf16),
             pltpu.VMEM((PAD_DATES, local_rows * LANES), f32),
             pltpu.VMEM((HALVES, per_half, PAD_DATES, LANES), bf16),
-            pltpu.VMEM((n, PAD_DATES, LANES), bf16),
             pltpu.VMEM((16, 256), bf16),
             pltpu.VMEM((n, 16, 256), bf16),
-            pltpu.VMEM((8, n * LANES), f32),
+            pltpu.SemaphoreType.REGULAR((2,)),
             dma((2, HALVES)),
             dma((2, HALVES)),
             dma((HALVES, per_half)),
@@ -593,15 +597,24 @@
             collective_id=0, has_side_effects=True, vmem_limit_bytes=RAISED
         ),
     )(
-        interferograms,
+        interferograms.reshape(images * local_rows, columns),
         pseudo_inverse,
         date_pairs,
         ref_pixel,
         band_width,
-        prior_mean,
-        prior_precision,
-        jnp.asarray(trend),
     )
+    return pl.pallas_call(
+        functools.partial(finish, n, gram.tolist()),
+        out_shape=(
+            jax.ShapeDtypeStruct((1, DATES, n * LANES), bf16),
+            jax.ShapeDtypeStruct((1, 4, n * LANES), f32),
+            jax.ShapeDtypeStruct((1, n * LANES), bf16),
+        ),
+        in_specs=[vmem] * 5,
+        out_specs=(vmem, vmem, vmem),
+        scratch_shapes=[pltpu.VMEM((8, n * LANES), f32)],
+        compiler_params=pltpu.CompilerParams(vmem_limit_bytes=RAISED // 2),
+    )(arrived, ref_sum, prior_mean, prior_precision, jnp.asarray(trend))
 
 
 def on_device(

time: 63.2 us -> 59.4 us (0.940)
  local copies, waits for them, and re-layouts: 4.79 us -> 1.88 us
    unnamed x3 -> x10, local copies, waits for them, and re-layouts: 4.79 us -> 1.88 us
    pallas_call x1 -> x2, Pallas kernels: 55.7 us -> 55.2 us  [the longest x1 54 us: in_kernel(): pl.pallas_call(functools.partial(kernel, n), out_shape=(jax.ShapeDtypeStr...]
where the time goes in v3:
time: 59.4 us; the launch traced here: 59 us
  Pallas kernels  55.2 us (93%)
  between operations  2 us (3%)
  local copies, waits for them, and re-layouts  1.88 us (3%)
    pallas_call x1, Pallas kernels, in_kernel(): pl.pallas_call(functools.partial(kernel, n), out_shape=(jax.ShapeDtypeStr...  54 us
    unnamed x10, local copies, waits for them, and re-layouts  1.88 us

profile of v3, /device:TPU:1, one launch (start us, length us, event | category | flops | bytes accessed | tf_op | source)
XLA Modules:
  0.0 59.0 jit_solution(1536597983061347136)
XLA Ops:
  0.6 0.0 copy-start.4
  0.6 0.0 copy-start.2
  0.7 0.0 copy-start.1
  2.0 54.0 %shard_map.103 = (bf16[16,208,128]{2,1,0:T(8,128)(2,1)}, f32[16,256]{1,0:T(8,128)}) custom-call(bf16[4800,256]{1,0:T(8,128)(2,1)} %bitcast.1, bf16[200,600]{1,0:T(8,128)(2,1)} %pinv_ref.1, s32[2,600]{1,0:T(2,128)} %pairs_ref.1, s32[1]{0:T(128)S(6)} %copy.11.pixel_ref, s32[1]{0:T(128)S(6)} %copy.12.band_ref), custom_call_target="tpu_custom_call" | custom-call | tf_op jit(solution)/shard_map/pallas_call | solution.py:566
  56.0 0.0 copy-done.4
  56.0 0.0 copy-done.2
  56.0 0.0 copy-done.1
  56.0 0.0 copy-start
  56.0 1.1 %copy-done = bf16[16,208,128]{2,1,0:T(8,128)(2,1)S(1)} copy-done((bf16[16,208,128]{2,1,0:T(8,128)(2,1)S(1)}, bf16[16,208,128]{2,1,0:T(8,128)(2,1)}, u32[]{:S(2)}) %copy-start) | copy-done | bytes 851992
  57.1 0.0 copy-start.3
  57.1 0.7 %copy-done.3 = f32[16,256]{1,0:T(8,128)S(1)} copy-done((f32[16,256]{1,0:T(8,128)S(1)}, f32[16,256]{1,0:T(8,128)}, u32[]{:S(2)}) %copy-start.3) | copy-done | bytes 16408
  57.9 1.2 %shard_map.104 = (bf16[1,200,2048]{2,1,0:T(8,128)(2,1)}, f32[1,4,2048]{2,1,0:T(4,128)}, bf16[1,2048]{1,0:T(2,128)(2,1)}) custom-call(bf16[16,208,128]{2,1,0:T(8,128)(2,1)S(1)} %copy-done, f32[16,256]{1,0:T(8,128)S(1)} %copy-done.3, f32[1,4,2048]{2,1,0:T(4,128)S(1)} %copy-done.1, f32[1,4,2048]{2,1,0:T(4,128)S(1)} %copy-done.2, bf16[16,208]{1,0:T(8,128)(2,1)S(1)} %copy-done.4), custom_call_target="tpu_custom_call" | custom-call | tf_op jit(solution)/shard_map/pallas_call | solution.py:606
Async XLA Ops:
  0.6 55.3 %copy-start.4 = (bf16[16,208]{1,0:T(8,128)(2,1)S(1)}, bf16[16,208]{1,0:T(8,128)(2,1)}, u32[]{:S(2)}) copy-start(bf16[16,208]{1,0:T(8,128)(2,1)} %constant.2.clone.trend_ref) | copy-start | bytes 19972
  0.6 55.3 %copy-start.2 = (f32[1,4,2048]{2,1,0:T(4,128)S(1)}, f32[1,4,2048]{2,1,0:T(4,128)}, u32[]{:S(2)}) copy-start(f32[1,4,2048]{2,1,0:T(4,128)} %precision_ref.1) | copy-start | bytes 98308
  0.7 55.3 %copy-start.1 = (f32[1,4,2048]{2,1,0:T(4,128)S(1)}, f32[1,4,2048]{2,1,0:T(4,128)}, u32[]{:S(2)}) copy-start(f32[1,4,2048]{2,1,0:T(4,128)} %mean_ref.1) | copy-start | bytes 98308
  56.0 1.2 %copy-start = (bf16[16,208,128]{2,1,0:T(8,128)(2,1)S(1)}, bf16[16,208,128]{2,1,0:T(8,128)(2,1)}, u32[]{:S(2)}) copy-start(bf16[16,208,128]{2,1,0:T(8,128)(2,1)} %get-tuple-element.5.arrived) | copy-start | bytes 2555908
  57.1 0.7 %copy-start.3 = (f32[16,256]{1,0:T(8,128)S(1)}, f32[16,256]{1,0:T(8,128)}, u32[]{:S(2)}) copy-start(f32[16,256]{1,0:T(8,128)} %get-tuple-element.6.ref_sum) | copy-start | bytes 49156

commit v4 on v3

--- a/solution.py
+++ b/solution.py
@@ -178,6 +178,7 @@
 PAD_DEPTH = 640
 PAD_DATES = 208
 LANES = 128
+FINISH = 8
 GROUP = 32
 UNROLL = True
 HALVES = 2
@@ -515,9 +516,9 @@
         ref_copy(k).wait_send()
 
 
-def finish(n, gram, arrived, ref_sum, mean_ref, precision_ref, trend_ref, series_ref, state_ref, misfit_ref, proj):
+def finish(gram, arrived, ref_sum, mean_ref, precision_ref, trend_ref, series_ref, state_ref, misfit_ref, proj):
     ref_column = jnp.broadcast_to(ref_sum[0:1], (LANES, 256)).T[0:PAD_DATES]
-    for j in range(n):
+    for j in range(arrived.shape[0]):
         values = arrived[j].astype(jnp.float32)
         lanes = slice(j * LANES, (j + 1) * LANES)
         series = (values - ref_column).astype(jnp.bfloat16)
@@ -604,15 +605,26 @@
         band_width,
     )
     return pl.pallas_call(
-        functools.partial(finish, n, gram.tolist()),
+        functools.partial(finish, gram.tolist()),
         out_shape=(
             jax.ShapeDtypeStruct((1, DATES, n * LANES), bf16),
             jax.ShapeDtypeStruct((1, 4, n * LANES), f32),
             jax.ShapeDtypeStruct((1, n * LANES), bf16),
         ),
-        in_specs=[vmem] * 5,
-        out_specs=(vmem, vmem, vmem),
-        scratch_shapes=[pltpu.VMEM((8, n * LANES), f32)],
+        grid=(n // FINISH,),
+        in_specs=[
+            pl.BlockSpec((FINISH, PAD_DATES, LANES), lambda g: (g, 0, 0)),
+            vmem,
+            pl.BlockSpec((1, 4, FINISH * LANES), lambda g: (0, 0, g)),
+            pl.BlockSpec((1, 4, FINISH * LANES), lambda g: (0, 0, g)),
+            vmem,
+        ],
+        out_specs=(
+            pl.BlockSpec((1, DATES, FINISH * LANES), lambda g: (0, 0, g)),
+            pl.BlockSpec((1, 4, FINISH * LANES), lambda g: (0, 0, g)),
+            pl.BlockSpec((1, FINISH * LANES), lambda g: (0, g)),
+        ),
+        scratch_shapes=[pltpu.VMEM((8, FINISH * LANES), f32)],
         compiler_params=pltpu.CompilerParams(vmem_limit_bytes=RAISED // 2),
     )(arrived, ref_sum, prior_mean, prior_precision, jnp.asarray(trend))
 

time: 59.4 us -> 59.6 us (level)
  no operation moved by 1% of the time
where the time goes in v4:
time: 59.6 us; the launch traced here: 59.2 us
  Pallas kernels  55.3 us (93%)
  between operations  2 us (3%)
  local copies, waits for them, and re-layouts  1.88 us (3%)
    pallas_call x1, Pallas kernels, in_kernel(): pl.pallas_call(functools.partial(kernel, n), out_shape=(jax.ShapeDtypeStr...  54 us
    unnamed x10, local copies, waits for them, and re-layouts  1.88 us
    pallas_call x1, Pallas kernels, in_kernel(): pl.pallas_call(functools.partial(finish, gram.tolist()), out_shape=(jax.S...  1.37 us

profile of v4, /device:TPU:1, one launch (start us, length us, event | category | flops | bytes accessed | tf_op | source)
XLA Modules:
  0.0 59.2 jit_solution(9345397310363485199)
XLA Ops:
  0.6 0.0 copy-start.4
  0.6 0.0 copy-start.2
  0.7 0.0 copy-start.1
  2.0 54.0 %shard_map.103 = (bf16[16,208,128]{2,1,0:T(8,128)(2,1)}, f32[16,256]{1,0:T(8,128)}) custom-call(bf16[4800,256]{1,0:T(8,128)(2,1)} %bitcast.1, bf16[200,600]{1,0:T(8,128)(2,1)} %pinv_ref.1, s32[2,600]{1,0:T(2,128)} %pairs_ref.1, s32[1]{0:T(128)S(6)} %copy.11.pixel_ref, s32[1]{0:T(128)S(6)} %copy.12.band_ref), custom_call_target="tpu_custom_call" | custom-call | tf_op jit(solution)/shard_map/pallas_call | solution.py:567
  56.0 0.0 copy-done.4
  56.0 0.0 copy-done.2
  56.0 0.0 copy-done.1
  56.0 0.0 copy-start
  56.0 1.1 %copy-done = bf16[16,208,128]{2,1,0:T(8,128)(2,1)S(1)} copy-done((bf16[16,208,128]{2,1,0:T(8,128)(2,1)S(1)}, bf16[16,208,128]{2,1,0:T(8,128)(2,1)}, u32[]{:S(2)}) %copy-start) | copy-done | bytes 851992
  57.1 0.0 copy-start.3
  57.1 0.7 %copy-done.3 = f32[16,256]{1,0:T(8,128)S(1)} copy-done((f32[16,256]{1,0:T(8,128)S(1)}, f32[16,256]{1,0:T(8,128)}, u32[]{:S(2)}) %copy-start.3) | copy-done | bytes 16408
  57.9 1.4 %shard_map.104 = (bf16[1,200,2048]{2,1,0:T(8,128)(2,1)}, f32[1,4,2048]{2,1,0:T(4,128)}, bf16[1,2048]{1,0:T(2,128)(2,1)}) custom-call(bf16[16,208,128]{2,1,0:T(8,128)(2,1)S(1)} %copy-done, f32[16,256]{1,0:T(8,128)S(1)} %copy-done.3, f32[1,4,2048]{2,1,0:T(4,128)S(1)} %copy-done.1, f32[1,4,2048]{2,1,0:T(4,128)S(1)} %copy-done.2, bf16[16,208]{1,0:T(8,128)(2,1)S(1)} %copy-done.4), custom_call_target="tpu_custom_call" | custom-call | tf_op jit(solution)/shard_map/pallas_call | solution.py:607
Async XLA Ops:
  0.6 55.3 %copy-start.4 = (bf16[16,208]{1,0:T(8,128)(2,1)S(1)}, bf16[16,208]{1,0:T(8,128)(2,1)}, u32[]{:S(2)}) copy-start(bf16[16,208]{1,0:T(8,128)(2,1)} %constant.2.clone.trend_ref) | copy-start | bytes 19972
  0.6 55.3 %copy-start.2 = (f32[1,4,2048]{2,1,0:T(4,128)S(1)}, f32[1,4,2048]{2,1,0:T(4,128)}, u32[]{:S(2)}) copy-start(f32[1,4,2048]{2,1,0:T(4,128)} %precision_ref.1) | copy-start | bytes 98308
  0.7 55.3 %copy-start.1 = (f32[1,4,2048]{2,1,0:T(4,128)S(1)}, f32[1,4,2048]{2,1,0:T(4,128)}, u32[]{:S(2)}) copy-start(f32[1,4,2048]{2,1,0:T(4,128)} %mean_ref.1) | copy-start | bytes 98308
  56.0 1.2 %copy-start = (bf16[16,208,128]{2,1,0:T(8,128)(2,1)S(1)}, bf16[16,208,128]{2,1,0:T(8,128)(2,1)}, u32[]{:S(2)}) copy-start(bf16[16,208,128]{2,1,0:T(8,128)(2,1)} %get-tuple-element.5.arrived) | copy-start | bytes 2555908
  57.1 0.7 %copy-start.3 = (f32[16,256]{1,0:T(8,128)S(1)}, f32[16,256]{1,0:T(8,128)}, u32[]{:S(2)}) copy-start(f32[16,256]{1,0:T(8,128)} %get-tuple-element.6.ref_sum) | copy-start | bytes 49156
